TPU v7x, 32 devices: a whole 2x2x4 slice. The times are simulated.
32 devices in a mesh: tower: 2 (over core), rows: 16 (over z, y, x).
Axes of the slice: x: 2, y: 2, z: 4, core: 2. Of those that a mesh axis runs over, the one named last changes fastest.
Arguments:
- tokens: bfloat16 [2, 32, 512, 512], P('tower', 'rows'), may hold values from -9 to 9
- segment_ids: int32 [2, 32, 512], P('tower', 'rows'), may hold values from 0 to 8, never falling along the last dimension, each value on 1 to 128 neighbouring positions
- positives: int32 [256], P('rows'), may hold values from 0 to 255, each once
- attention_gain: float32 [512], replicated, may hold values from 0.5 to 1.5
- query_weight: bfloat16 [512, 512], replicated, may hold values from -0.0625 to 0.0625
- key_weight: bfloat16 [512, 512], replicated, may hold values from -0.25 to 0.25
- value_weight: bfloat16 [512, 512], replicated, may hold values from -0.25 to 0.25
- output_weight: bfloat16 [512, 512], replicated, may hold values from -1 to 1
- position_table: float32 [32, 8], replicated, may hold values from -3 to 3
- feedforward_gain: float32 [512], replicated, may hold values from 0.5 to 1.5
- inner_weight: bfloat16 [512, 2048], replicated, may hold values from -0.25 to 0.25
- outer_weight: bfloat16 [2048, 512], replicated, may hold values from -0.1875 to 0.1875
Outputs:
- layer_output: bfloat16 [2, 32, 512, 512], P('tower', 'rows')
- token_grad: bfloat16 [2, 32, 512, 512], P('tower', 'rows')
- attention_gain_grad: float32 [512], replicated
- query_grad: float32 [512, 512], replicated
- key_grad: float32 [512, 512], replicated
- value_grad: float32 [512, 512], replicated
- output_grad: float32 [512, 512], replicated
- position_grad: float32 [32, 8], replicated
- feedforward_gain_grad: float32 [512], replicated
- inner_grad: float32 [512, 2048], replicated
- outer_grad: float32 [2048, 512], replicated
- contrastive_loss: float32 [], replicated
- root_mean_squares: float32 [3], replicated
Inputs may be any that keep to these rules, and one draw needn't show every extreme that they name: `segment_ids`: within each row of 512 tokens the numbers never fall; 0 to 7 are the row's items and 8 marks the padding at its end; every number, padding included, covers 1 to 128 tokens. positives[m] is the document item paired with query item m; every document item occurs once.
All inputs are finite; a program needn't handle non-finite values.
Results may differ from a plain program's by a relative error of at most 0.028.
The roundings to bfloat16 on the way count: a program that leaves them out, or rounds other values in their place, can miss the bound.
Values sent between devices are 32-bit elements; how exact they have to be, the bound alone decides.
A program may use at most 320 MiB of HBM per device.

v0:
```python
import functools
import math

import jax
import jax.numpy as jnp
import numpy as np
from jax import lax
from jax.experimental import pallas as pl
from jax.experimental.pallas import tpu as pltpu
from jax.sharding import PartitionSpec as P

MAX_DIST = 128
ITEMS_ROW = 8


EPSILON = 1e-06
SOFTMAX_TEMP = 0.01
LOSS_SCALE = 65536.0
MATMUL_PRECISION = lax.Precision.HIGHEST


def from_partner(value, axis, apart):
    mask = 2**apart
    pairs = [(source, source ^ mask) for source in range(lax.axis_size(axis))]
    return lax.ppermute(value, axis, pairs)


def bucket_table(length, bucket_count, far_limit):
    half_count = bucket_count // 2
    exact_count = half_count // 2
    entries = []
    for offset in range(1 - length, length):
        distance = abs(offset)
        if distance < exact_count:
            within = distance
        else:
            within = exact_count + int(
                math.log(distance / exact_count)
                / math.log(far_limit / exact_count)
                * (half_count - exact_count)
            )
            within = min(within, half_count - 1)
        entries.append(within + (half_count if offset > 0 else 0))
    by_offset = np.array(entries, dtype=np.int32)
    index_grid = np.arange(length)[None, :] - np.arange(length)[:, None] + length - 1
    return (by_offset, by_offset[index_grid])


def contract_rows(left_side, right_side):
    return lax.dot_general(
        left_side, right_side, (((0,), (0,)), ((), ())), preferred_element_type=jnp.float32
    )


def times_transpose(left_side, right_side):
    return lax.dot_general(
        left_side, right_side, (((1,), (1,)), ((), ())), preferred_element_type=jnp.float32
    )


def norm_scale(values):
    return lax.rsqrt(jnp.mean(values * values, axis=1, keepdims=True) + EPSILON)


def norm_back(grad_normed, values, scale, gain):
    gained = grad_normed * gain
    return scale * (
        gained - values * scale * scale * jnp.mean(gained * values, axis=1, keepdims=True)
    )


def row_scores(query_part, key_part, segment_row, position_bias, head_count):
    length = query_part.shape[0]
    query_heads = query_part.reshape(length, head_count, -1)
    key_heads = key_part.reshape(length, head_count, -1)
    scores = (
        jnp.einsum("qhd,khd->hqk", query_heads, key_heads, preferred_element_type=jnp.float32)
        + position_bias
    )
    same_item = segment_row[:, None] == segment_row[None, :]
    return jnp.where(same_item[None], scores, -1e30)


def diagonal_sums(square):
    head_count = square.shape[0]
    length = square.shape[1]
    flipped = square[:, :, ::-1]
    padded = jnp.pad(flipped, ((0, 0), (0, 0), (0, length)))
    sheared = padded.reshape(head_count, 2 * length * length)[:, : length * (2 * length - 1)]
    sheared = sheared.reshape(head_count, length, 2 * length - 1)
    return jnp.sum(sheared, axis=1)[:, ::-1]


def shards(
    tokens,
    segment_ids,
    positives,
    attention_gain,
    query_weight,
    key_weight,
    value_weight,
    output_weight,
    position_table,
    feedforward_gain,
    inner_weight,
    outer_weight,
):
    row_count = tokens.shape[1]
    length = tokens.shape[2]
    model_width = tokens.shape[3]
    head_count = position_table.shape[1]
    inner_width = query_weight.shape[1]
    head_size = inner_width // head_count
    token_count = row_count * length
    by_offset, bucket_index = bucket_table(length, position_table.shape[0], MAX_DIST)
    position_bias = jnp.take(position_table.T, jnp.asarray(bucket_index), axis=1)
    inputs = tokens.reshape(token_count, model_width).astype(jnp.float32)
    segments = segment_ids.reshape(row_count, length)
    scale_one = norm_scale(inputs)
    normed_one = (inputs * scale_one * attention_gain).astype(jnp.bfloat16)
    query_rows = jnp.dot(normed_one, query_weight, preferred_element_type=jnp.float32).astype(
        jnp.bfloat16
    )
    key_rows = jnp.dot(normed_one, key_weight, preferred_element_type=jnp.float32).astype(
        jnp.bfloat16
    )
    value_rows = jnp.dot(normed_one, value_weight, preferred_element_type=jnp.float32).astype(
        jnp.bfloat16
    )
    query_blocks = query_rows.reshape(row_count, length, inner_width)
    key_blocks = key_rows.reshape(row_count, length, inner_width)
    value_blocks = value_rows.reshape(row_count, length, inner_width)

    def attend(packed):
        query_part, key_part, value_part, segment_row = packed
        scores = row_scores(query_part, key_part, segment_row, position_bias, head_count)
        highest = jnp.max(scores, axis=2, keepdims=True)
        exp_scores = jnp.exp(scores - highest)
        exp_total = jnp.sum(exp_scores, axis=2, keepdims=True)
        attention_probs = (exp_scores / exp_total).astype(jnp.bfloat16)
        value_heads = value_part.reshape(length, head_count, head_size)
        mixed_heads = jnp.einsum(
            "hqk,khd->qhd", attention_probs, value_heads, preferred_element_type=jnp.float32
        )
        return (
            mixed_heads.reshape(length, inner_width).astype(jnp.bfloat16),
            (highest + jnp.log(exp_total))[:, :, 0],
        )

    mixed_blocks, log_totals = lax.map(attend, (query_blocks, key_blocks, value_blocks, segments))
    mixed_rows = mixed_blocks.reshape(token_count, inner_width)
    branch_one = jnp.dot(mixed_rows, output_weight, preferred_element_type=jnp.float32)
    middle = inputs + branch_one
    scale_two = norm_scale(middle)
    normed_two = (middle * scale_two * feedforward_gain).astype(jnp.bfloat16)
    hidden = jax.nn.relu(
        jnp.dot(normed_two, inner_weight, preferred_element_type=jnp.float32)
    ).astype(jnp.bfloat16)
    branch_two = jnp.dot(hidden, outer_weight, preferred_element_type=jnp.float32)
    result = middle + branch_two
    valid_mask = (segments < ITEMS_ROW).astype(jnp.float32).reshape(token_count, 1)
    stat_terms = jnp.stack(
        [
            jnp.sum(valid_mask * result * result),
            jnp.sum(valid_mask * branch_one * branch_one),
            jnp.sum(valid_mask * branch_two * branch_two),
            jnp.sum(valid_mask),
        ]
    )
    stat_totals = lax.psum(stat_terms, ("tower", "rows"))
    member = (segments[:, None, :] == jnp.arange(ITEMS_ROW)[None, :, None]).astype(jnp.float32)
    item_sizes = jnp.sum(member, axis=2, keepdims=True)
    result_blocks = result.reshape(row_count, length, model_width)
    pooled = (
        jnp.einsum("ris,rsd->rid", member, result_blocks, precision=MATMUL_PRECISION) / item_sizes
    )
    items_here = row_count * ITEMS_ROW
    pooled = pooled.reshape(items_here, model_width)
    inverse_norm = lax.rsqrt(jnp.sum(pooled * pooled, axis=1, keepdims=True) + EPSILON)
    embedded_tokens = pooled * inverse_norm
    tower_index = lax.axis_index("tower")
    is_query = tower_index == 0
    partner = from_partner(embedded_tokens, "tower", 0)
    query_vectors = jnp.where(is_query, embedded_tokens, partner)
    document_vectors = jnp.where(is_query, partner, embedded_tokens)
    gathered_documents = lax.all_gather(document_vectors, "rows", axis=0, tiled=True)
    item_total = gathered_documents.shape[0]
    half_items = items_here // 2
    my_queries = lax.dynamic_slice_in_dim(query_vectors, tower_index * half_items, half_items, 0)
    my_targets = lax.dynamic_slice_in_dim(positives, tower_index * half_items, half_items, 0)
    similarity_scores = (
        lax.dot_general(
            my_queries,
            gathered_documents,
            (((1,), (1,)), ((), ())),
            precision=MATMUL_PRECISION,
            preferred_element_type=jnp.float32,
        )
        / SOFTMAX_TEMP
    )
    highest = jnp.max(similarity_scores, axis=1, keepdims=True)
    exp_logits = jnp.exp(similarity_scores - highest)
    exp_total = jnp.sum(exp_logits, axis=1, keepdims=True)
    log_total = highest[:, 0] + jnp.log(exp_total[:, 0])
    is_target = jnp.arange(item_total)[None, :] == my_targets[:, None]
    target = jnp.sum(jnp.where(is_target, similarity_scores, 0.0), axis=1)
    loss_part = jnp.sum(log_total - target)
    similarity_gradient = (exp_logits / exp_total - is_target.astype(jnp.float32)) * (
        LOSS_SCALE / item_total
    )
    local_gradient = (
        jnp.dot(similarity_gradient, gathered_documents, precision=MATMUL_PRECISION) / SOFTMAX_TEMP
    )
    grad_documents = lax.psum_scatter(
        lax.dot_general(
            similarity_gradient,
            my_queries,
            (((0,), (0,)), ((), ())),
            precision=MATMUL_PRECISION,
            preferred_element_type=jnp.float32,
        )
        / SOFTMAX_TEMP,
        "rows",
        scatter_dimension=0,
        tiled=True,
    )
    partner_mine, partner_documents = from_partner((local_gradient, grad_documents), "tower", 0)
    query_side = jnp.where(
        is_query,
        jnp.concatenate([local_gradient, partner_mine], 0),
        jnp.concatenate([partner_mine, local_gradient], 0),
    )
    own_grad = jnp.where(is_query, query_side, grad_documents + partner_documents)
    inner_along = jnp.sum(own_grad * embedded_tokens, axis=1, keepdims=True)
    grad_pooled = inverse_norm * (own_grad - embedded_tokens * inner_along)
    per_token = grad_pooled.reshape(row_count, ITEMS_ROW, model_width) / item_sizes
    grad_result = jnp.einsum("ris,rid->rsd", member, per_token, precision=MATMUL_PRECISION).reshape(
        token_count, model_width
    )
    grad_branch_two = grad_result.astype(jnp.bfloat16)
    outer_grad = contract_rows(hidden, grad_branch_two)
    grad_hidden = times_transpose(grad_branch_two, outer_weight)
    grad_pre = jnp.where(hidden > 0, grad_hidden, 0.0).astype(jnp.bfloat16)
    inner_grad = contract_rows(normed_two, grad_pre)
    grad_normed_two = times_transpose(grad_pre, inner_weight)
    feedforward_gain_grad = jnp.sum(grad_normed_two * middle * scale_two, axis=0)
    grad_middle = grad_result + norm_back(grad_normed_two, middle, scale_two, feedforward_gain)
    grad_branch_one = grad_middle.astype(jnp.bfloat16)
    output_grad = contract_rows(mixed_rows, grad_branch_one)
    grad_mixed = times_transpose(grad_branch_one, output_weight).astype(jnp.bfloat16)
    grad_mixed_blocks = grad_mixed.reshape(row_count, length, inner_width)

    def attend_back(running, packed):
        query_part, key_part, value_part, segment_row, row_log_total, grad_part = packed
        scores = row_scores(query_part, key_part, segment_row, position_bias, head_count)
        attention_probs = jnp.exp(scores - row_log_total[:, :, None])
        query_heads = query_part.reshape(length, head_count, head_size)
        key_heads = key_part.reshape(length, head_count, head_size)
        value_heads = value_part.reshape(length, head_count, head_size)
        grad_heads = grad_part.reshape(length, head_count, head_size)
        grad_value = jnp.einsum(
            "hqk,qhd->khd",
            attention_probs.astype(jnp.bfloat16),
            grad_heads,
            preferred_element_type=jnp.float32,
        )
        grad_probs = jnp.einsum(
            "qhd,khd->hqk", grad_heads, value_heads, preferred_element_type=jnp.float32
        )
        row_dot = jnp.sum(attention_probs * grad_probs, axis=2, keepdims=True)
        grad_scores = (attention_probs * (grad_probs - row_dot)).astype(jnp.bfloat16)
        grad_query = jnp.einsum(
            "hqk,khd->qhd", grad_scores, key_heads, preferred_element_type=jnp.float32
        )
        grad_key = jnp.einsum(
            "hqk,qhd->khd", grad_scores, query_heads, preferred_element_type=jnp.float32
        )
        outputs = (
            grad_query.reshape(length, inner_width).astype(jnp.bfloat16),
            grad_key.reshape(length, inner_width).astype(jnp.bfloat16),
            grad_value.reshape(length, inner_width).astype(jnp.bfloat16),
        )
        return (running + grad_scores.astype(jnp.float32), outputs)

    score_sum, grad_rows = lax.scan(
        attend_back,
        jnp.zeros((head_count, length, length), jnp.float32),
        (query_blocks, key_blocks, value_blocks, segments, log_totals, grad_mixed_blocks),
    )
    grad_queries = grad_rows[0].reshape(token_count, inner_width)
    grad_keys = grad_rows[1].reshape(token_count, inner_width)
    grad_values = grad_rows[2].reshape(token_count, inner_width)
    query_grad = contract_rows(normed_one, grad_queries)
    key_grad = contract_rows(normed_one, grad_keys)
    value_grad = contract_rows(normed_one, grad_values)
    grad_normed_one = (
        times_transpose(grad_queries, query_weight)
        + times_transpose(grad_keys, key_weight)
        + times_transpose(grad_values, value_weight)
    )
    attention_gain_grad = jnp.sum(grad_normed_one * inputs * scale_one, axis=0)
    token_grad = grad_middle + norm_back(grad_normed_one, inputs, scale_one, attention_gain)
    offset_onehot = jnp.asarray(
        (by_offset[:, None] == np.arange(position_table.shape[0])[None, :]).astype(np.float32)
    )
    position_grad = jnp.dot(diagonal_sums(score_sum), offset_onehot, precision=MATMUL_PRECISION).T
    closing_terms = loss_part[None]
    summed = lax.psum(
        (
            attention_gain_grad,
            query_grad,
            key_grad,
            value_grad,
            output_grad,
            position_grad,
            feedforward_gain_grad,
            inner_grad,
            outer_grad,
            closing_terms,
        ),
        ("tower", "rows"),
    )
    (
        attention_gain_grad,
        query_grad,
        key_grad,
        value_grad,
        output_grad,
        position_grad,
        feedforward_gain_grad,
        inner_grad,
        outer_grad,
        closing_totals,
    ) = summed
    contrastive_loss = closing_totals[0] / item_total
    root_mean_squares = jnp.sqrt(stat_totals[:3] / (stat_totals[3] * model_width))
    block_shape = (1, row_count, length, model_width)
    return (
        result.reshape(block_shape).astype(jnp.bfloat16),
        token_grad.reshape(block_shape).astype(jnp.bfloat16),
        attention_gain_grad,
        query_grad,
        key_grad,
        value_grad,
        output_grad,
        position_grad,
        feedforward_gain_grad,
        inner_grad,
        outer_grad,
        contrastive_loss,
        root_mean_squares,
    )


F32 = jnp.float32
BF = jnp.bfloat16
MESH = pl.DeviceIdType.MESH
NN = (((1,), (0,)), ((), ()))
NT = (((1,), (1,)), ((), ()))
TN = (((0,), (0,)), ((), ()))
WIDE = 128
UNITS = 4096 // WIDE
PER_PART = 256 // WIDE
STEPS_AFTER = (
    (),
    (0, 1, 2, 3,),
    (4, 5, 6, 7,),
    (8, 9, 10, 11, 0, 1,),
    (12, 13, 14, 15, 2, 3,),
    (),
    (4, 5, 0, 1,),
    (6, 7, 2, 3,),
    (8, 9,),
    (10, 11, 4, 5, 16, 17, 18, 19,),
    (12, 13, 14, 15, 6, 7, 8,),
    (9, 10, 0, 1, 2, 3,),
    (11, 12,),
    (13,),
    (14,),
    (15, 20, 21,),
    (22, 23, 24, 25, 4, 5, 0, 1, 2, 3,),
    (16, 17,),
    (6, 7, 8, 9, 11, 10, 18, 19, 4, 5, 13, 12, 0,),
    (14, 15, 1, 2, 20, 21, 3,),
    (),
    (6, 7,),
    (26, 27, 22, 23, 8, 9, 11, 28,),
    (29, 30, 31, 24, 25, 10, 13, 16, 17, 4, 5,),
    (12, 14, 15, 18, 19, 6, 21, 0, 7, 1, 2,),
    (20, 8, 9, 11, 10, 3,),
    (26, 27, 22, 23, 13, 16,),
    (28, 29, 12, 14, 15, 17, 0, 18, 30, 31, 1, 32, 19, 25, 24, 5, 4, 2, 21, 7, 6, 9, 8, 11, 10, 20, 3, 27, 26, 13, 22, 28, 29, 12, 23, 15, 14, 16, 30, 17, 18, 0, 19, 31, 1, 0, 32, 25, 5, 1, 24, 3, 4, 2, 16, 3, 21, 17, 18, 7, 2, 32, 19, 6, 9, 8, 5, 4, 11, 5, 10, 4, 17, 16, 20, 21, 17, 16, 27, 7, 26, 13, 18, 7, 19, 22, 18, 28, 6, 19, 29, 9, 12, 6, 8, 9, 23, 15, 11, 14, 20, 8, 10, 11, 30, 10, 21, 31, 12, 25, 23, 32, 24, 21, 13, 12, 22, 27, 13, 14, 26, 28, 15, 14, 20, 29, 32, 30, 25, 15, 23, 20, 31, 24, 22, 23, 26, 27, 28, 22, 29, 30, 31, 25, 24, 25, 27, 24, 26, 27, 29, 26, 28, 29, 31, 28, 30, 31, 30,),
)
SMALL = UNITS
PIECES = len(STEPS_AFTER)
FAR = 512
NEAR = 384
WINDOWS = ((0, 256, 128), (0, 384, 0), (128, 384, 0), (256, 256, 0))


def dot(a, b, dims=NN):
    return lax.dot_general(a, b, dims, preferred_element_type=F32)


def exact_dot(a, b, dims=NN):
    return lax.dot_general(
        a, b, dims, precision=lax.Precision.HIGHEST, preferred_element_type=F32
    )


def tile(index, size):
    if isinstance(index, int):
        return pl.ds(index * size, size)
    return pl.ds(pl.multiple_of(index * size, size), size)


def far_limits(bucket_count, far_limit):
    half_count = bucket_count // 2
    exact_count = half_count // 2
    limits = []
    reached = exact_count
    for distance in range(exact_count, 512):
        within = exact_count + int(
            math.log(distance / exact_count)
            / math.log(far_limit / exact_count)
            * (half_count - exact_count)
        )
        within = min(within, half_count - 1)
        while reached < within:
            limits.append(distance)
            reached += 1
    return limits


def bucket_onehot(offset):
    distance = jnp.abs(offset)
    far = jnp.full_like(distance, 8)
    for limit in far_limits(32, MAX_DIST):
        far = far + jnp.where(distance >= limit, 1, 0)
    bucket = jnp.where(distance < 8, distance, far) + jnp.where(offset > 0, 16, 0)
    same = bucket == lax.broadcasted_iota(jnp.int32, (32, FAR), 0)
    return jnp.where(same, 1.0, 0.0).astype(F32)


def split_three(value):
    high = value.astype(BF)
    rest = value - high.astype(F32)
    middle = rest.astype(BF)
    return high, middle, (rest - middle.astype(F32)).astype(BF)


class Place:
    def __init__(self):
        self.tower = lax.axis_index("tower")
        self.rows = lax.axis_index("rows")
        self.flat = lax.rem(self.rows, 4)
        self.deep = lax.div(self.rows, 4)
        bits = {
            "x": lax.rem(self.rows, 2),
            "y": lax.rem(lax.div(self.rows, 2), 2),
            "z": lax.rem(lax.div(self.rows, 4), 2),
            "w": lax.div(self.rows, 8),
        }
        steps = {"x": 1, "y": 2, "z": 4, "w": 8}
        self.bit = {"c": self.tower, **bits}
        self.to = {"c": self.device(1 - self.tower, self.rows)}
        for name, step in steps.items():
            self.to[name] = self.device(self.tower, self.rows + step * (1 - 2 * bits[name]))

    def device(self, tower, rows):
        return {"tower": tower, "rows": rows}

    def along_deep(self, step):
        return self.device(self.tower, lax.rem(self.deep + step, 4) * 4 + self.flat)

    def along_flat(self, step):
        return self.device(self.tower, self.deep * 4 + lax.rem(self.flat + step, 4))


def order_of(unit):
    return (("cxzyw", "cyzxw") if unit < UNITS // 2 else ("cxyZ", "cyxZ"))[unit % 2]


class Sums:
    def __init__(self, place, total, landed, out, small, small_landed, sems):
        self.place, self.total, self.landed, self.out = place, total, landed, out
        self.small, self.small_landed = small, small_landed
        self.send_sem, self.recv_sem, self.out_sem, self.small_send, self.small_recv = sems
        self.plans = {}
        self.stage = {}
        for unit in range(UNITS):
            order = order_of(unit)
            if order not in self.plans:
                self.plans[order] = self.plan(order)

    def plan(self, order):
        place, steps = self.place, []
        base, size, offset, sem = 0, 512, 0, 0
        for name in order:
            ways = 4 if name == "Z" else 2
            size //= ways
            spot = place.deep if name == "Z" else place.bit[name]
            partners = []
            for i in range(1, ways):
                if name == "Z":
                    piece, device = lax.rem(place.deep + i, 4), place.along_deep(i)
                else:
                    piece, device = 1 - spot, place.to[name]
                partners.append((base + piece * size, device, offset, sem))
                offset, sem = offset + size, sem + 1
            base = base + spot * size
            steps.append((size, base, partners))
        return steps

    def remote(self, source, target, index, unit, device):
        return pltpu.make_async_remote_copy(
            src_ref=source,
            dst_ref=target,
            send_sem=self.send_sem.at[index, unit],
            recv_sem=self.recv_sem.at[index, unit],
            device_id=device,
            device_id_type=MESH,
        )

    def depth(self, unit):
        return 5 if unit == SMALL else 2 * len(order_of(unit))

    def rows(self, start, size):
        return pl.ds(pl.multiple_of(start, size), size)

    def keep(self, unit):
        size, base, _ = self.plans[order_of(unit)][-1]
        rows = self.rows(base, size)
        return pltpu.make_async_copy(
            self.total.at[unit, rows], self.out.at[unit, rows], self.out_sem.at[unit]
        )

    def copies(self, stage, unit):
        if unit == SMALL:
            return [
                pltpu.make_async_remote_copy(
                    src_ref=self.small,
                    dst_ref=self.small_landed.at[stage],
                    send_sem=self.small_send.at[stage],
                    recv_sem=self.small_recv.at[stage],
                    device_id=self.place.to["cxyzw"[stage]],
                    device_id_type=MESH,
                )
            ]
        plan = self.plans[order_of(unit)]
        if stage < len(plan):
            size, _, partners = plan[stage]
            return [
                self.remote(
                    self.total.at[unit, self.rows(start, size)],
                    self.landed.at[unit, pl.ds(offset, size)],
                    sem,
                    unit,
                    device,
                )
                for start, device, offset, sem in partners
            ]
        back = 2 * len(plan) - 1 - stage
        size, base, partners = plan[back]
        rows = self.rows(base, size)
        source = self.total if stage == len(plan) else self.out
        return [
            self.remote(source.at[unit, rows], self.out.at[unit, rows], 6 + sem, unit, device)
            for _, device, _, sem in partners
        ]

    def step(self, unit):
        stage = self.stage.get(unit, -1)
        plan = None if unit == SMALL else self.plans[order_of(unit)]
        if stage >= 0:
            for copy in self.copies(stage, unit):
                copy.wait()
            if unit == SMALL:
                self.small[...] += self.small_landed[stage]
            elif stage < len(plan):
                size, base, partners = plan[stage]
                parts = [self.landed[unit, pl.ds(p[2], size), :] for p in partners]
                self.total[unit, self.rows(base, size), :] += sum(parts[1:], parts[0])
            elif stage == len(plan):
                self.keep(unit).wait()
        stage += 1
        self.stage[unit] = stage
        if stage < self.depth(unit):
            for copy in self.copies(stage, unit):
                copy.start()
            if plan is not None and stage == len(plan):
                self.keep(unit).start()

    def fill(self, part, value):
        for i in range(PER_PART):
            self.total[part * PER_PART + i] = value[:, i * WIDE : (i + 1) * WIDE]

    def after(self, piece, *parts):
        for part in parts:
            for i in range(PER_PART):
                self.step(part * PER_PART + i)
        if piece == PIECES - 1:
            self.step(SMALL)
        for unit in STEPS_AFTER[piece]:
            self.step(unit)


class Spread:
    def __init__(self, place, blocks, send_sem, recv_sem):
        self.place, self.blocks = place, blocks
        self.send_sem, self.recv_sem = send_sem, recv_sem

    def copy(self, row, index, where, device):
        ref = self.blocks.at[where]
        return pltpu.make_async_remote_copy(
            src_ref=ref,
            dst_ref=ref,
            send_sem=self.send_sem.at[row, index],
            recv_sem=self.recv_sem.at[row, index],
            device_id=device,
            device_id_type=MESH,
        )

    def one(self, row, i):
        place = self.place
        where = (row, place.tower, place.deep, place.flat)
        return self.copy(row, i, where, place.along_deep(i + 1))

    def copies(self, row, stage):
        place = self.place
        if stage == 0:
            return [self.one(row, i) for i in range(3)]
        if stage == 1:
            where = (row, place.tower, slice(None), place.flat)
            return [self.copy(row, 3 + i, where, place.along_flat(i + 1)) for i in range(3)]
        return [self.copy(row, 6, (row, place.tower), place.to["c"])]

    def start(self, row, stage):
        for copy in self.copies(row, stage):
            copy.start()

    def wait(self, row, stage):
        for copy in self.copies(row, stage):
            copy.wait()


def layer_kernel(
    tokens_hbm,
    segment_ref,
    positive_ref,
    gain_one_ref,
    query_hbm,
    key_hbm,
    value_hbm,
    output_hbm,
    table_ref,
    gain_two_ref,
    inner_hbm,
    outer_hbm,
    layer_hbm,
    token_grad_hbm,
    sums_hbm,
    hidden_sum_hbm,
    rows_grad_hbm,
    small_ref,
    tokens,
    query_w,
    key_w,
    value_w,
    output_w,
    inner_w,
    outer_w,
    normed_one,
    queries,
    keys,
    values,
    probs,
    side_probs,
    mixed,
    middle,
    normed_two,
    hidden,
    bias,
    segment_column,
    segment_row,
    pooled_all,
    hidden_sum,
    normed_one_t,
    normed_two_t,
    mixed_t,
    grad_mixed,
    grad_query,
    grad_key,
    grad_value,
    key_total,
    value_total,
    total,
    landed,
    expand,
    rounded_grads,
    small_landed,
    load_sem,
    store_sem,
    sum_send,
    sum_recv,
    sum_out,
    pool_send,
    pool_recv,
    hidden_send,
    hidden_recv,
    small_send,
    small_recv,
    relay_send,
    relay_recv,
):
    place = Place()
    barrier = pltpu.get_barrier_semaphore()
    partners = [place.to["c"]]
    partners += [place.along_deep(i) for i in (1, 2, 3)]
    partners += [place.along_flat(i) for i in (1, 2, 3)]
    for partner in partners:
        pl.semaphore_signal(barrier, inc=1, device_id=partner, device_id_type=MESH)

    loads = [
        pltpu.make_async_copy(source, target, load_sem.at[i])
        for i, (source, target) in enumerate(
            (
                (tokens_hbm, tokens),
                (query_hbm, query_w),
                (key_hbm, key_w),
                (value_hbm, value_w),
                (output_hbm, output_w),
                (inner_hbm, inner_w),
                (outer_hbm, outer_w),
            )
        )
    ]
    for load in loads:
        load.start()

    segment_row[...] = segment_ref[...].astype(F32)
    for i in range(8):
        row = segment_row[i // 4 : i // 4 + 1, (i % 4) * 128 : (i % 4) * 128 + 128]
        segment_column[i * 128 : (i + 1) * 128, :] = jnp.broadcast_to(row, (128, 128)).T
    place_row = lax.broadcasted_iota(jnp.int32, (32, FAR), 1)
    offsets = jnp.where(place_row >= NEAR, place_row - FAR, place_row) - 128
    by_place = exact_dot(table_ref[...], bucket_onehot(offsets))
    for h in range(8):
        spread = jnp.broadcast_to(by_place[h : h + 1], (128, FAR))
        bias[h] = pltpu.roll(spread, 0, 1, stride=1, stride_axis=0)[:, :NEAR]
    pooling = Spread(place, pooled_all, pool_send, pool_recv)
    sums = Sums(
        place,
        total,
        landed,
        sums_hbm,
        small_ref,
        small_landed,
        (sum_send, sum_recv, sum_out, small_send, small_recv),
    )

    def hidden_slot(row):
        return hidden_sum_hbm.at[row, place.tower, place.deep, place.bit["y"], place.bit["x"]]

    def save_hidden(row):
        return pltpu.make_async_copy(hidden_sum.at[row], hidden_slot(row), store_sem.at[row])

    def hidden_copy(source, target, row, index, device):
        return pltpu.make_async_remote_copy(
            src_ref=source,
            dst_ref=target,
            send_sem=hidden_send.at[row, index],
            recv_sem=hidden_recv.at[row, index],
            device_id=device,
            device_id_type=MESH,
        )

    def go(copies, start):
        for copy in copies:
            if start:
                copy.start()
            else:
                copy.wait()

    def deepen_hidden(row, start):
        source = hidden_sum.at[row]
        target = hidden_slot(row)
        copies = [
            hidden_copy(source, target, row, i - 1, place.along_deep(i)) for i in (1, 2, 3)
        ]
        go(copies, start)

    def widen_hidden(row, step, start):
        ref = hidden_sum_hbm.at[row, place.tower]
        y, x = place.bit["y"], place.bit["x"]
        left, right = pl.ds(0, 1024), pl.ds(1024, 1024)
        if step == 0:
            parts = (ref.at[:, y, x, :, left], "x"), (ref.at[:, y, x, :, right], "y")
        else:
            parts = (ref.at[:, y, :, :, left], "y"), (ref.at[:, :, x, :, right], "x")
        copies = [
            hidden_copy(part, part, row, 3 + 2 * step + i, place.to[name])
            for i, (part, name) in enumerate(parts)
        ]
        go(copies, start)

    def swap_hidden(row, start):
        ref = hidden_sum_hbm.at[row, place.tower]
        go([hidden_copy(ref, ref, row, 7, place.to["c"])], start)

    def relay(step, start):
        ref = pooled_all.at[1, place.tower, lax.rem(place.deep + 4 - step, 4), place.flat]
        copies = [
            pltpu.make_async_remote_copy(
                src_ref=ref,
                dst_ref=ref,
                send_sem=relay_send.at[step, i - 1],
                recv_sem=relay_recv.at[step, i - 1],
                device_id=place.along_flat(i),
                device_id_type=MESH,
            )
            for i in (1, 2, 3)
        ]
        go(copies, start)

    head_lane = lax.broadcasted_iota(jnp.int32, (1, 256), 1) // 64
    head_mask = [jnp.where(head_lane == h, 1.0, 0.0) for h in range(4)]
    head_mask_low = [mask.astype(BF) for mask in head_mask]

    def stack_heads(part):
        return jnp.concatenate([part * mask for mask in head_mask_low], 0)

    def pick_heads(part):
        return sum(part[h * 128 : (h + 1) * 128] * head_mask[h] for h in range(4))

    def project(i, carry):
        rows = tile(i, 256)
        x = tokens[rows, :].astype(F32)
        scale = lax.rsqrt(jnp.mean(x * x, axis=1, keepdims=True) + EPSILON)
        normed = (x * scale * gain_one_ref[...]).astype(BF)
        normed_one[rows, :] = normed
        queries[rows, :] = dot(normed, query_w[...]).astype(BF)
        keys[rows, :] = dot(normed, key_w[...]).astype(BF)
        values[rows, :] = dot(normed, value_w[...]).astype(BF)
        return carry

    def window(r, b):
        start, width, offset = WINDOWS[b]
        base = r * 512
        own = pl.ds(pl.multiple_of(base + b * 128, 128), 128)
        near = pl.ds(pl.multiple_of(base + start, 128), width)
        return own, near, slice(start, start + width), slice(offset, offset + width)

    def soft(r, b, g):
        if b in (0, 3):
            return side_probs.at[r, b // 3, g]
        return probs.at[r, b - 1, g]

    def attend(b, r, carry):
        own, near, near_row, offset = window(r, b)
        column = segment_column[own, :]
        row = segment_row[pl.ds(r, 1), near_row]
        same = jnp.concatenate([column] * (WINDOWS[b][1] // 128), 1) == row
        for g in range(2):
            lanes = slice(g * 256, (g + 1) * 256)
            scores = dot(stack_heads(queries[own, lanes]), keys[near, lanes], NT)
            parts = []
            for h in range(4):
                part = scores[h * 128 : (h + 1) * 128] + bias[g * 4 + h, :, offset]
                part = jnp.where(same, part, -1e30)
                highest = jnp.max(part, axis=1, keepdims=True)
                exp_part = jnp.exp(part - highest)
                exp_total = jnp.sum(exp_part, axis=1, keepdims=True)
                parts.append((exp_part * (1.0 / exp_total)).astype(BF))
            stacked = jnp.concatenate(parts, 0)
            soft(r, b, g)[...] = stacked
            mixed[own, lanes] = pick_heads(dot(stacked, values[near, lanes])).astype(BF)
        return carry

    def feed(i, carry):
        rows = tile(i, 256)
        branch = dot(mixed[rows, :], output_w[...])
        mid = tokens[rows, :].astype(F32) + branch
        middle[rows, :] = mid
        scale = lax.rsqrt(jnp.mean(mid * mid, axis=1, keepdims=True) + EPSILON)
        normed = (mid * scale * gain_two_ref[...]).astype(BF)
        normed_two[rows, :] = normed
        for c in range(4):
            lanes = slice(c * 512, (c + 1) * 512)
            hidden[rows, lanes] = jnp.maximum(dot(normed, inner_w[:, lanes]), 0.0).astype(BF)
        valid = jnp.where(segment_column[rows, 0:1] < ITEMS_ROW, 1.0, 0.0)
        small_ref[3:4, :] += jnp.sum(valid * branch * branch, axis=0, keepdims=True)
        small_ref[5:6, :] += jnp.sum(valid * jnp.ones_like(branch), axis=0, keepdims=True)
        return carry

    def pool(r):
        rows = tile(r, 512)
        number = lax.broadcasted_iota(jnp.int32, (8, 512), 0).astype(F32)
        member = jnp.where(segment_row[pl.ds(r, 1), :] == number, 1.0, 0.0)
        member_low = jnp.concatenate([member, jnp.zeros_like(member)], 0).astype(BF)
        count = jnp.sum(member, axis=1, keepdims=True)
        hidden_part = dot(member_low, hidden[rows, :])[:8]
        hidden_sum[r] = hidden_part
        middle_part = exact_dot(member, middle[rows, :])
        pieces = split_three(hidden_part)
        stacked = jnp.concatenate([*pieces, jnp.zeros_like(pieces[0])], 0)
        branch = dot(stacked, outer_w[...])
        pooled = (middle_part + (branch[0:8] + branch[8:16] + branch[16:24])) / count
        sublane = lax.broadcasted_iota(jnp.int32, (8, 128), 0)
        ids = jnp.zeros((8, 128), F32)
        for s in range(8):
            ids = jnp.where(sublane == s, positive_ref[r * 8 + s].astype(F32), ids)
        lanes = lax.broadcasted_iota(jnp.int32, (8, 128), 1)
        extra = jnp.where(lanes == 0, ids, count)
        pooled_all[r, place.tower, place.deep, place.flat] = jnp.concatenate([pooled, extra], 1)

    small_ref[...] = jnp.zeros_like(small_ref)
    for i in range(4):
        loads[i].wait()
    pl.semaphore_wait(barrier, len(partners))

    def forward(r, carry):
        first, second = r == 0, r == 1
        lax.fori_loop(2 * r, 2 * r + 2, project, 0)
        attend(0, r, 0)
        attend(1, r, 0)

        @pl.when(second)
        def _():
            pooling.wait(0, 0)
            pooling.start(0, 1)

        attend(2, r, 0)
        attend(3, r, 0)

        @pl.when(first)
        def _():
            for i in (4, 5):
                loads[i].wait()

        @pl.when(second)
        def _():
            save_hidden(0).wait()
            deepen_hidden(0, start=False)
            widen_hidden(0, 0, start=True)

        lax.fori_loop(2 * r, 2 * r + 2, feed, 0)

        @pl.when(first)
        def _():
            loads[6].wait()

        @pl.when(second)
        def _():
            pooling.wait(0, 1)
            pooling.start(0, 2)

        pool(r)
        pooling.start(r, 0)

        @pl.when(second)
        def _():
            relay(0, start=True)

        deepen_hidden(r, start=True)
        save_hidden(r).start()
        return carry

    lax.fori_loop(0, 2, forward, 0)

    def store_rows(source, target, i, index):
        rows = tile(i, 256)
        return pltpu.make_async_copy(source.at[rows], target.at[rows], store_sem.at[index])

    def close(i, carry):
        rows = tile(i, 256)
        branch = dot(hidden[rows, :], outer_w[...])
        result = middle[rows, :] + branch
        grad_query[rows, :] = result.astype(BF)
        valid = jnp.where(segment_column[rows, 0:1] < ITEMS_ROW, 1.0, 0.0)
        small_ref[2:3, :] += jnp.sum(valid * result * result, axis=0, keepdims=True)
        small_ref[4:5, :] += jnp.sum(valid * branch * branch, axis=0, keepdims=True)
        return carry

    def turn(i, carry):
        rows = tile(i, 128)
        normed_two_t[:, rows] = normed_two[rows, :].T
        mixed_t[:, rows] = mixed[rows, :].T
        normed_one_t[:, rows] = normed_one[rows, :].T
        return carry

    lax.fori_loop(0, 3, close, 0)
    for step in (1, 2, 3):
        if step == 3:
            lax.fori_loop(3, 4, close, 0)
        pooling.one(1, step - 1).wait()
        relay(step, start=True)
    for i in range(4):
        store_rows(grad_query, layer_hbm, i, 2 + i).start()
    save_hidden(1).wait()
    lax.fori_loop(0, 8, turn, 0)
    widen_hidden(0, 0, start=False)
    widen_hidden(0, 1, start=True)
    lane = lax.broadcasted_iota(jnp.int32, (1, 128), 1)
    item = segment_column[...] + jnp.where(
        lax.broadcasted_iota(jnp.int32, (1024, 128), 0) >= 512, 8.0, 0.0
    )
    item = jnp.where(segment_column[...] < ITEMS_ROW, item, -1.0)
    slot = jnp.where(lane < 48, lax.rem(lane, 16), -2).astype(F32)
    expand[...] = jnp.where(item == slot, 1.0, 0.0).astype(BF)
    for step in range(4):
        relay(step, start=False)
    pooling.start(1, 2)
    deepen_hidden(1, start=False)
    widen_hidden(1, 0, start=True)
    pooling.wait(0, 2)
    pooling.wait(1, 2)

    gathered = [
        jnp.concatenate([pooled_all[r, t].reshape(128, 640) for r in range(2)], 0)
        for t in range(2)
    ]
    vectors, inverse, counts, embedded = [], [], [], []
    for t in range(2):
        vector = gathered[t][:, :512]
        scale = lax.rsqrt(jnp.sum(vector * vector, axis=1, keepdims=True) + EPSILON)
        vectors.append(vector)
        inverse.append(scale)
        embedded.append(vector * scale)
        counts.append(gathered[t][:, 513:514])
    logits = exact_dot(embedded[0], embedded[1], NT) / SOFTMAX_TEMP
    highest = jnp.max(logits, axis=1, keepdims=True)
    exp_logits = jnp.exp(logits - highest)
    exp_total = jnp.sum(exp_logits, axis=1, keepdims=True)
    position = lax.broadcasted_iota(jnp.int32, (256, 256), 1)
    number = lax.rem(lax.div(position, 8), 16) * 16 + lax.div(position, 128) * 8
    number = (number + lax.rem(position, 8)).astype(F32)
    is_target = gathered[0][:, 512:513] == number
    target = jnp.sum(jnp.where(is_target, logits, 0.0), axis=1, keepdims=True)
    losses = highest + jnp.log(exp_total) - target
    loss = jnp.sum(losses, axis=0, keepdims=True) / 256
    grad_logits = (exp_logits / exp_total - jnp.where(is_target, 1.0, 0.0)) * (LOSS_SCALE / 256)
    grads = (
        exact_dot(grad_logits, embedded[1]) / SOFTMAX_TEMP,
        exact_dot(grad_logits, embedded[0], TN) / SOFTMAX_TEMP,
    )
    for t in range(2):
        along = jnp.sum(grads[t] * embedded[t], axis=1, keepdims=True)
        per_token = inverse[t] * (grads[t] - embedded[t] * along) / counts[t]
        for r in range(2):
            part = per_token[r * 128 : (r + 1) * 128]
            for i in range(512 // WIDE):
                total[UNITS - 4 + 2 * r + t, i * 128 : (i + 1) * 128] = part[
                    :, i * WIDE : (i + 1) * WIDE
                ]
            rounded_grads[r, t] = per_token[r * 128 : (r + 1) * 128].astype(BF)
    save_grads = pltpu.make_async_copy(rounded_grads, rows_grad_hbm, store_sem.at[6])
    save_grads.start()
    own_parts = []
    for r in range(2):
        spot = UNITS - 4 + 2 * r + place.tower
        lanes = [total[spot, tile(place.rows + 16 * i, 8)] for i in range(512 // WIDE)]
        own_parts.append(jnp.concatenate(lanes, 1))
    own = jnp.concatenate(own_parts, 0)
    pieces = split_three(own)
    own_low = pieces[0]
    own_split = jnp.concatenate([*pieces, jnp.zeros((80, 512), BF)], 0)

    def back_hidden(c):
        lanes = slice(c * 512, (c + 1) * 512)
        row_part = dot(own_low, outer_w[lanes, :], NT).astype(BF)
        row_part = jnp.concatenate([row_part, jnp.zeros((112, 512), BF)], 0)

        def mask(i, carry):
            rows = tile(i, 256)
            spread = dot(expand[rows, :], row_part)
            hidden[rows, lanes] = jnp.where(hidden[rows, lanes] > 0, spread, 0.0).astype(BF)
            return carry

        lax.fori_loop(0, 4, mask, 0)
        for half in range(2):
            part = 2 * c + half
            columns = slice(part * 256, (part + 1) * 256)
            sums.fill(part, dot(normed_two_t[...], hidden[:, columns]))
        sums.after(c, 2 * c, 2 * c + 1)

    def back_middle(i, carry):
        rows = tile(i, 256)
        grad_normed = dot(hidden[rows, :], inner_w[...], NT)
        mid = middle[rows, :]
        scale = lax.rsqrt(jnp.mean(mid * mid, axis=1, keepdims=True) + EPSILON)
        small_ref[1:2, :] += jnp.sum(grad_normed * mid * scale, axis=0, keepdims=True)
        gained = grad_normed * gain_two_ref[...]
        mean = jnp.mean(gained * mid, axis=1, keepdims=True)
        grad_mid = dot(expand[rows, :], own_split) + scale * (gained - mid * scale * scale * mean)
        middle[rows, :] = grad_mid
        rounded = grad_mid.astype(BF)
        mixed[rows, :] = rounded
        grad_mixed[rows, :] = dot(rounded, output_w[...], NT).astype(BF)
        return carry

    for c in range(4):
        back_hidden(c)
    for i in range(2):
        lax.fori_loop(2 * i, 2 * i + 2, back_middle, 0)
        sums.after(4 + 2 * i)
        sums.after(5 + 2 * i)
    for half in range(2):
        sums.fill(8 + half, dot(mixed_t[...], mixed[:, half * 256 : (half + 1) * 256]))
    widen_hidden(1, 0, start=False)
    widen_hidden(1, 1, start=True)
    sums.after(8, 8, 9)

    for i in range(4):
        store_rows(grad_query, layer_hbm, i, 2 + i).wait()
    bias[...] = jnp.zeros_like(bias)

    def attend_back(g, b, r, carry):
        own, near, _, offset = window(r, b)
        lanes = slice(g * 256, (g + 1) * 256)
        grad_stack = stack_heads(grad_mixed[own, lanes])
        grad_soft = dot(grad_stack, values[near, lanes], NT)
        weight = soft(r, b, g)[...]
        parts = []
        for h in range(4):
            rows = slice(h * 128, (h + 1) * 128)
            soft_part = weight[rows].astype(F32)
            grad_part = grad_soft[rows]
            along = jnp.sum(soft_part * grad_part, axis=1, keepdims=True)
            part = (soft_part * (grad_part - along)).astype(BF)
            bias[g * 4 + h, :, offset] += part.astype(F32)
            parts.append(part)
        stacked = jnp.concatenate(parts, 0)
        grad_query[own, lanes] = pick_heads(dot(stacked, keys[near, lanes])).astype(BF)
        key_total[near, :] += dot(stacked, stack_heads(queries[own, lanes]), TN)
        value_total[near, :] += dot(weight, grad_stack, TN)
        return carry

    for g in range(2):
        lanes = slice(g * 256, (g + 1) * 256)
        key_total[...] = jnp.zeros_like(key_total)
        value_total[...] = jnp.zeros_like(value_total)
        for b in range(4):
            lax.fori_loop(0, 2, functools.partial(attend_back, g, b), 0)
            sums.after(9 + 7 * g + b)
        part, piece = 10 + 3 * g, 13 + 7 * g
        sums.fill(part, dot(normed_one_t[...], grad_query[:, lanes]))
        sums.after(piece, part)
        grad_key[:, lanes] = key_total[...].astype(BF)
        sums.fill(part + 1, dot(normed_one_t[...], grad_key[:, lanes]))
        sums.after(piece + 1, part + 1)
        grad_value[:, lanes] = value_total[...].astype(BF)
        sums.fill(part + 2, dot(normed_one_t[...], grad_value[:, lanes]))
        sums.after(piece + 2, part + 2)
        if g == 0:
            widen_hidden(0, 1, start=False)
            swap_hidden(0, start=True)
    widen_hidden(1, 1, start=False)
    swap_hidden(0, start=False)
    swap_hidden(1, start=True)

    def back_tokens(i, carry):
        rows = tile(i, 256)
        grad_normed = (
            dot(grad_query[rows, :], query_w[...], NT)
            + dot(grad_key[rows, :], key_w[...], NT)
            + dot(grad_value[rows, :], value_w[...], NT)
        )
        x = tokens[rows, :].astype(F32)
        scale = lax.rsqrt(jnp.mean(x * x, axis=1, keepdims=True) + EPSILON)
        small_ref[0:1, :] += jnp.sum(grad_normed * x * scale, axis=0, keepdims=True)
        gained = grad_normed * gain_one_ref[...]
        mean = jnp.mean(gained * x, axis=1, keepdims=True)
        grad = middle[rows, :] + scale * (gained - x * scale * scale * mean)
        normed_one[rows, :] = grad.astype(BF)
        return carry

    for i in range(2):
        lax.fori_loop(2 * i, 2 * i + 2, back_tokens, 0)
        for j in (2 * i, 2 * i + 1):
            store_rows(normed_one, token_grad_hbm, j, 2 + j).start()
            sums.after(23 + j)
    mirror = (
        lax.broadcasted_iota(jnp.int32, (128, 128), 0)
        + lax.broadcasted_iota(jnp.int32, (128, 128), 1)
    )
    mirror = jnp.where(mirror == 127, 1.0, 0.0)
    diagonals = []
    for h in range(8):
        turned = exact_dot(mirror, bias[h])
        wide = jnp.concatenate([turned, jnp.zeros((128, FAR - NEAR), F32)], 1)
        wide = pltpu.roll(wide, 0, 1, stride=1, stride_axis=0)
        diagonals.append(jnp.sum(wide, axis=0, keepdims=True))
    buckets = exact_dot(jnp.concatenate(diagonals, 0), bucket_onehot(place_row - 255), NT)
    small_ref[8:16, :] = jnp.concatenate([buckets, jnp.zeros((8, 480), F32)], 1)
    sums.after(27)
    small_ref[6:7, :] = jnp.broadcast_to(loss, (1, 512))
    swap_hidden(1, start=False)
    save_grads.wait()
    for i in range(4):
        store_rows(normed_one, token_grad_hbm, i, 2 + i).wait()


def closing_kernel(
    layer_hbm,
    token_grad_hbm,
    sums_hbm,
    hidden_sum_hbm,
    rows_grad_hbm,
    small_ref,
    layer_out,
    token_out,
    gain_one_out,
    query_out,
    key_out,
    value_out,
    output_out,
    position_out,
    gain_two_out,
    inner_out,
    outer_out,
    loss_out,
    square_out,
    hidden_sum,
    rows_grad,
    hidden_low,
    outer_part,
    rows_part,
    units_part,
    load_sem,
    copy_sem,
    store_sem,
):
    pairs = []
    inner_units = 2048 // WIDE
    for unit in range(inner_units):
        pairs.append((units_part.at[unit], inner_out.at[:, pl.ds(unit * WIDE, WIDE)]))
    places = [(output_out, 0), (output_out, 256)]
    places += [(ref, g * 256) for g in range(2) for ref in (query_out, key_out, value_out)]
    for part, (ref, lane) in enumerate(places):
        for i in range(PER_PART):
            lanes = pl.ds(lane + i * WIDE, WIDE)
            pairs.append((units_part.at[inner_units + part * PER_PART + i], ref.at[:, lanes]))
    pairs += [(rows_part.at[0], layer_out), (rows_part.at[1], token_out)]
    copies = [
        pltpu.make_async_copy(source, target, copy_sem.at[i])
        for i, (source, target) in enumerate(pairs)
    ]
    pairs = [(rows_grad_hbm, rows_grad), (hidden_sum_hbm, hidden_sum)]
    pairs += [(sums_hbm.at[unit], units_part.at[unit]) for unit in range(UNITS)]
    pairs += [(layer_hbm, rows_part.at[0]), (token_grad_hbm, rows_part.at[1])]
    loads = [
        pltpu.make_async_copy(source, target, load_sem.at[i])
        for i, (source, target) in enumerate(pairs)
    ]
    for load in loads:
        load.start()
    gain_one_out[...] = small_ref[0, :]
    gain_two_out[...] = small_ref[1, :]
    position_out[...] = small_ref[8:16, 0:32]
    loss_out[0] = jnp.max(small_ref[6:7, :])
    squares = jnp.sum(small_ref[2:5, :], axis=1, keepdims=True)
    valid = jnp.sum(small_ref[5:6, :], axis=1, keepdims=True)
    roots = jnp.sqrt(squares / valid)
    for i in range(3):
        square_out[i] = jnp.max(roots[i : i + 1, :])
    loads[0].wait()
    loads[1].wait()
    hidden_low[...] = hidden_sum[...].reshape(512, 2048).astype(BF)
    grads = rows_grad[...].reshape(512, 512)
    stores = []
    for c in range(4):
        rows = pl.ds(c * 512, 512)
        outer_part[rows] = dot(hidden_low[:, c * 512 : (c + 1) * 512], grads, TN)
        store = pltpu.make_async_copy(outer_part.at[rows], outer_out.at[rows], store_sem.at[c])
        store.start()
        stores.append(store)
        for i in range(UNITS // 4 * c, UNITS // 4 * (c + 1)):
            loads[2 + i].wait()
            copies[i].start()
    for i in (UNITS, UNITS + 1):
        loads[2 + i].wait()
        copies[i].start()
    for copy in copies + stores:
        copy.wait()


def fast_shards(
    tokens,
    segment_ids,
    positives,
    attention_gain,
    query_weight,
    key_weight,
    value_weight,
    output_weight,
    position_table,
    feedforward_gain,
    inner_weight,
    outer_weight,
):
    block_shape = tokens.shape
    anywhere = pl.BlockSpec(memory_space=pl.ANY)
    vmem = pl.BlockSpec(memory_space=pltpu.VMEM)
    smem = pl.BlockSpec(memory_space=pltpu.SMEM)
    shape = jax.ShapeDtypeStruct
    dma = pltpu.SemaphoreType.DMA
    low = functools.partial(pltpu.VMEM, dtype=BF)
    full = functools.partial(pltpu.VMEM, dtype=F32)
    outs = pl.pallas_call(
        layer_kernel,
        out_shape=[
            shape((1024, 512), BF),
            shape((1024, 512), BF),
            shape((UNITS, 512, WIDE), F32),
            shape((2, 2, 4, 2, 2, 8, 2048), F32),
            shape((2, 2, 128, 512), BF),
            shape((16, 512), F32),
        ],
        in_specs=[anywhere, vmem, smem, vmem]
        + [anywhere] * 4
        + [vmem, vmem, anywhere, anywhere],
        out_specs=[anywhere] * 5 + [vmem],
        scratch_shapes=[
            low((1024, 512)),
            low((512, 512)),
            low((512, 512)),
            low((512, 512)),
            low((512, 512)),
            low((512, 2048)),
            low((2048, 512)),
            low((1024, 512)),
            low((1024, 512)),
            low((1024, 512)),
            low((1024, 512)),
            low((2, 2, 2, 512, 384)),
            low((2, 2, 2, 512, 256)),
            low((1024, 512)),
            full((1024, 512)),
            low((1024, 512)),
            low((1024, 2048)),
            full((8, 128, NEAR)),
            full((1024, 128)),
            full((2, 512)),
            full((2, 2, 4, 4, 8, 640)),
            full((2, 8, 2048)),
            low((512, 1024)),
            low((512, 1024)),
            low((512, 1024)),
            low((1024, 512)),
            low((1024, 512)),
            low((1024, 512)),
            low((1024, 512)),
            full((1024, 256)),
            full((1024, 256)),
            full((UNITS, 512, WIDE)),
            full((UNITS, 496, WIDE)),
            low((1024, 128)),
            low((2, 2, 128, 512)),
            full((5, 16, 512)),
            dma((7,)),
            dma((7,)),
            dma((12, UNITS)),
            dma((12, UNITS)),
            dma((UNITS,)),
            dma((2, 7)),
            dma((2, 7)),
            dma((2, 8)),
            dma((2, 8)),
            dma((5,)),
            dma((5,)),
            dma((4, 3)),
            dma((4, 3)),
        ],
        compiler_params=pltpu.CompilerParams(
            collective_id=0, has_side_effects=True, vmem_limit_bytes=63 * 2**20
        ),
    )(
        tokens.reshape(1024, 512),
        segment_ids.reshape(2, 512),
        positives,
        attention_gain.reshape(1, 512),
        query_weight,
        key_weight,
        value_weight,
        output_weight,
        position_table.T,
        feedforward_gain.reshape(1, 512),
        inner_weight,
        outer_weight,
    )
    results = pl.pallas_call(
        closing_kernel,
        out_shape=[
            shape((1024, 512), BF),
            shape((1024, 512), BF),
            shape((512,), F32),
            shape((512, 512), F32),
            shape((512, 512), F32),
            shape((512, 512), F32),
            shape((512, 512), F32),
            shape((8, 32), F32),
            shape((512,), F32),
            shape((512, 2048), F32),
            shape((2048, 512), F32),
            shape((1,), F32),
            shape((3,), F32),
        ],
        in_specs=[anywhere] * 5 + [vmem],
        out_specs=[anywhere, anywhere, vmem]
        + [anywhere] * 4
        + [vmem, vmem, anywhere, anywhere, smem, smem],
        scratch_shapes=[
            full((2, 2, 4, 2, 2, 8, 2048)),
            low((2, 2, 128, 512)),
            low((512, 2048)),
            full((2048, 512)),
            low((2, 1024, 512)),
            full((UNITS, 512, WIDE)),
            dma((UNITS + 4,)),
            dma((UNITS + 2,)),
            dma((4,)),
        ],
        compiler_params=pltpu.CompilerParams(vmem_limit_bytes=60 * 2**20),
    )(*outs)
    layer, token_grad, *rest = results
    return (
        layer.reshape(block_shape),
        token_grad.reshape(block_shape),
        *rest[:5],
        rest[5].T,
        *rest[6:9],
        rest[9].reshape(()),
        rest[10],
    )


def solution(mesh):
    fast = mesh.shape["tower"] == 2 and mesh.shape["rows"] == 16
    return jax.shard_map(
        fast_shards if fast else shards,
        mesh=mesh,
        in_specs=(
            P("tower", "rows", None, None),
            P("tower", "rows", None),
            P("rows"),
            P(),
            P(),
            P(),
            P(),
            P(),
            P(),
            P(),
            P(),
            P(),
        ),
        out_specs=(
            P("tower", "rows", None, None),
            P("tower", "rows", None, None),
            P(),
            P(),
            P(),
            P(),
            P(),
            P(),
            P(),
            P(),
            P(),
            P(),
            P(),
        ),
        check_vma=False,
    )
```

profile of v0, /device:TPU:0, one launch (start us, length us, event | category | flops | bytes accessed | tf_op | source)
XLA Modules:
  0.0 145.1 jit_solution(2106835726730446556)
XLA Ops:
  0.6 132.6 %shard_map.219 = (bf16[1024,512]{1,0:T(8,128)(2,1)}, bf16[1024,512]{1,0:T(8,128)(2,1)}, f32[32,512,128]{2,1,0:T(8,128)}, f32[2,2,4,2,2,8,2048]{6,5,4,3,2,1,0:T(8...) custom-call(bf16[1024,512]{1,0:T(8,128)(2,1)} %bitcast.9, s32[2,512]{1,0:T(2,128)} %bitcast.10, ...), custom_call_target="tpu_custom_call" | custom-call | tf_op jit(solution)/shard_map/pallas_call | solution.py:1310
  133.3 11.6 %shard_map.220 = (bf16[1024,512]{1,0:T(8,128)(2,1)}, bf16[1024,512]{1,0:T(8,128)(2,1)}, f32[512]{0:T(512)}, f32[512,512]{1,0:T(8,128)}, f32[512,512]{1,0:T(8,128...) custom-call(bf16[1024,512]{1,0:T(8,128)(2,1)} %get-tuple-element.32., ...), custom_call_target="tpu_custom_call" | custom-call | tf_op jit(solution)/shard_map/pallas_call | solution.py:1392
where the time goes:
time: 145 us
  Pallas kernels  144 us (99%)
    pallas_call x1, Pallas kernels, fast_shards(): pl.pallas_call(layer_kernel, out_shape=[shape((1024, 512), BF), shape((10...  133 us
    pallas_call x1, Pallas kernels, fast_shards(): pl.pallas_call(closing_kernel, out_shape=[shape((1024, 512), BF), shape((...  11.6 us

commit v1 on v0

--- a/solution.py
+++ b/solution.py
@@ -366,30 +366,30 @@
     (0, 1, 2, 3,),
     (4, 5, 6, 7,),
     (8, 9, 10, 11, 0, 1,),
-    (12, 13, 14, 15, 2, 3,),
+    (12, 13, 2, 3, 14, 15,),
     (),
-    (4, 5, 0, 1,),
-    (6, 7, 2, 3,),
+    (0, 1, 4, 5,),
+    (2, 3, 6, 7,),
     (8, 9,),
-    (10, 11, 4, 5, 16, 17, 18, 19,),
-    (12, 13, 14, 15, 6, 7, 8,),
-    (9, 10, 0, 1, 2, 3,),
+    (4, 5, 10, 11, 16, 17, 18, 19,),
+    (6, 7, 12, 13, 8, 14, 15,),
+    (0, 1, 2, 3, 9, 10,),
     (11, 12,),
     (13,),
     (14,),
-    (15, 20, 21,),
-    (22, 23, 24, 25, 4, 5, 0, 1, 2, 3,),
+    (20, 15, 21,),
+    (0, 1, 2, 3, 4, 5, 22, 23, 24, 25,),
     (16, 17,),
-    (6, 7, 8, 9, 11, 10, 18, 19, 4, 5, 13, 12, 0,),
-    (14, 15, 1, 2, 20, 21, 3,),
+    (0, 6, 1, 7, 8, 9, 10, 11, 2, 18, 13, 12, 19,),
+    (3, 4, 5, 14, 15, 16, 17, 20, 21,),
     (),
-    (6, 7,),
-    (26, 27, 22, 23, 8, 9, 11, 28,),
-    (29, 30, 31, 24, 25, 10, 13, 16, 17, 4, 5,),
-    (12, 14, 15, 18, 19, 6, 21, 0, 7, 1, 2,),
-    (20, 8, 9, 11, 10, 3,),
-    (26, 27, 22, 23, 13, 16,),
-    (28, 29, 12, 14, 15, 17, 0, 18, 30, 31, 1, 32, 19, 25, 24, 5, 4, 2, 21, 7, 6, 9, 8, 11, 10, 20, 3, 27, 26, 13, 22, 28, 29, 12, 23, 15, 14, 16, 30, 17, 18, 0, 19, 31, 1, 0, 32, 25, 5, 1, 24, 3, 4, 2, 16, 3, 21, 17, 18, 7, 2, 32, 19, 6, 9, 8, 5, 4, 11, 5, 10, 4, 17, 16, 20, 21, 17, 16, 27, 7, 26, 13, 18, 7, 19, 22, 18, 28, 6, 19, 29, 9, 12, 6, 8, 9, 23, 15, 11, 14, 20, 8, 10, 11, 30, 10, 21, 31, 12, 25, 23, 32, 24, 21, 13, 12, 22, 27, 13, 14, 26, 28, 15, 14, 20, 29, 32, 30, 25, 15, 23, 20, 31, 24, 22, 23, 26, 27, 28, 22, 29, 30, 31, 25, 24, 25, 27, 24, 26, 27, 29, 26, 28, 29, 31, 28, 30, 31, 30,),
+    (6, 7, 22, 23, 8,),
+    (9, 18, 10, 26, 27, 28,),
+    (0, 1, 2, 3, 4, 11, 12, 13, 16, 17, 5, 19, 24, 25, 29, 30, 14, 31,),
+    (6, 7, 15, 18, 20, 8, 21, 22, 23,),
+    (0, 9, 10, 26, 27,),
+    (1, 2, 4, 5, 24, 28,),
+    (3, 11, 12, 13, 14, 15, 16, 17, 18, 19, 25, 29, 30, 7, 6, 20, 31, 32, 8, 21, 10, 22, 0, 26, 23, 4, 9, 5, 27, 0, 1, 16, 24, 28, 17, 2, 18, 1, 19, 11, 13, 25, 7, 15, 2, 3, 12, 6, 29, 14, 3, 31, 30, 20, 8, 32, 5, 21, 10, 16, 4, 18, 17, 5, 22, 4, 26, 7, 6, 23, 9, 20, 7, 32, 6, 27, 8, 24, 22, 21, 19, 28, 8, 11, 13, 10, 9, 23, 25, 15, 10, 24, 9, 12, 20, 21, 29, 14, 20, 22, 19, 21, 31, 11, 25, 30, 22, 16, 11, 18, 13, 24, 17, 13, 23, 24, 32, 26, 12, 23, 15, 27, 12, 14, 28, 29, 15, 19, 25, 14, 16, 32, 31, 25, 17, 30, 16, 18, 26, 27, 17, 28, 18, 29, 31, 19, 30, 19, 26, 27, 26, 28, 27, 29, 28, 30, 29, 31, 30, 31,),
 )
 SMALL = UNITS
 PIECES = len(STEPS_AFTER)
@@ -478,7 +478,7 @@
 
 
 def order_of(unit):
-    return (("cxzyw", "cyzxw") if unit < UNITS // 2 else ("cxyZ", "cyxZ"))[unit % 2]
+    return (("cxzyw", "cyzxw") if 8 * unit < 5 * UNITS else ("cxyZ", "cyxZ"))[unit % 2]
 
 
 class Sums:
@@ -925,42 +925,34 @@
         attend(0, r, 0)
         attend(1, r, 0)
 
+        attend(2, r, 0)
+        attend(3, r, 0)
+
+        @pl.when(first)
+        def _():
+            for i in (4, 5):
+                loads[i].wait()
+
         @pl.when(second)
         def _():
             pooling.wait(0, 0)
             pooling.start(0, 1)
 
-        attend(2, r, 0)
-        attend(3, r, 0)
+        lax.fori_loop(2 * r, 2 * r + 2, feed, 0)
 
         @pl.when(first)
         def _():
-            for i in (4, 5):
-                loads[i].wait()
+            loads[6].wait()
+
+        pool(r)
+        pooling.start(r, 0)
 
         @pl.when(second)
         def _():
+            relay(0, start=True)
             save_hidden(0).wait()
             deepen_hidden(0, start=False)
             widen_hidden(0, 0, start=True)
-
-        lax.fori_loop(2 * r, 2 * r + 2, feed, 0)
-
-        @pl.when(first)
-        def _():
-            loads[6].wait()
-
-        @pl.when(second)
-        def _():
-            pooling.wait(0, 1)
-            pooling.start(0, 2)
-
-        pool(r)
-        pooling.start(r, 0)
-
-        @pl.when(second)
-        def _():
-            relay(0, start=True)
 
         deepen_hidden(r, start=True)
         save_hidden(r).start()
@@ -995,6 +987,8 @@
             lax.fori_loop(3, 4, close, 0)
         pooling.one(1, step - 1).wait()
         relay(step, start=True)
+    pooling.wait(0, 1)
+    pooling.start(0, 2)
     for i in range(4):
         store_rows(grad_query, layer_hbm, i, 2 + i).start()
     save_hidden(1).wait()

time: 145 us -> 140 us (0.966)
  Pallas kernels: 144 us -> 139 us
    pallas_call x1, Pallas kernels: 133 us -> 127 us  [fast_shards(): pl.pallas_call(layer_kernel, out_shape=[shape((1024, 512), BF), shape((10...]
where the time goes in v1:
time: 140 us
  Pallas kernels  139 us (99%)
    pallas_call x1, Pallas kernels, fast_shards(): pl.pallas_call(layer_kernel, out_shape=[shape((1024, 512), BF), shape((10...  127 us
    pallas_call x1, Pallas kernels, fast_shards(): pl.pallas_call(closing_kernel, out_shape=[shape((1024, 512), BF), shape((...  11.6 us

profile of v1, /device:TPU:0, one launch (start us, length us, event | category | flops | bytes accessed | tf_op | source)
XLA Modules:
  0.0 139.7 jit_solution(2237867553931000699)
XLA Ops:
  0.6 127.2 %shard_map.219 = (bf16[1024,512]{1,0:T(8,128)(2,1)}, bf16[1024,512]{1,0:T(8,128)(2,1)}, f32[32,512,128]{2,1,0:T(8,128)}, f32[2,2,4,2,2,8,2048]{6,5,4,3,2,1,0:T(8...) custom-call(bf16[1024,512]{1,0:T(8,128)(2,1)} %bitcast.9, s32[2,512]{1,0:T(2,128)} %bitcast.10, ...), custom_call_target="tpu_custom_call" | custom-call | tf_op jit(solution)/shard_map/pallas_call | solution.py:1304
  127.9 11.6 %shard_map.220 = (bf16[1024,512]{1,0:T(8,128)(2,1)}, bf16[1024,512]{1,0:T(8,128)(2,1)}, f32[512]{0:T(512)}, f32[512,512]{1,0:T(8,128)}, f32[512,512]{1,0:T(8,128...) custom-call(bf16[1024,512]{1,0:T(8,128)(2,1)} %get-tuple-element.32., ...), custom_call_target="tpu_custom_call" | custom-call | tf_op jit(solution)/shard_map/pallas_call | solution.py:1386

commit v2 on v1

--- a/solution.py
+++ b/solution.py
@@ -888,9 +888,6 @@
         for c in range(4):
             lanes = slice(c * 512, (c + 1) * 512)
             hidden[rows, lanes] = jnp.maximum(dot(normed, inner_w[:, lanes]), 0.0).astype(BF)
-        valid = jnp.where(segment_column[rows, 0:1] < ITEMS_ROW, 1.0, 0.0)
-        small_ref[3:4, :] += jnp.sum(valid * branch * branch, axis=0, keepdims=True)
-        small_ref[5:6, :] += jnp.sum(valid * jnp.ones_like(branch), axis=0, keepdims=True)
         return carry
 
     def pool(r):
@@ -901,7 +898,7 @@
         count = jnp.sum(member, axis=1, keepdims=True)
         hidden_part = dot(member_low, hidden[rows, :])[:8]
         hidden_sum[r] = hidden_part
-        middle_part = exact_dot(member, middle[rows, :])
+        middle_part = sum(dot(member_low, piece) for piece in split_three(middle[rows, :]))[:8]
         pieces = split_three(hidden_part)
         stacked = jnp.concatenate([*pieces, jnp.zeros_like(pieces[0])], 0)
         branch = dot(stacked, outer_w[...])
@@ -915,6 +912,8 @@
         pooled_all[r, place.tower, place.deep, place.flat] = jnp.concatenate([pooled, extra], 1)
 
     small_ref[...] = jnp.zeros_like(small_ref)
+    in_item = jnp.where(segment_row[...] < ITEMS_ROW, 512.0, 0.0)
+    small_ref[5:6, :] = jnp.sum(in_item, axis=0, keepdims=True)
     for i in range(4):
         loads[i].wait()
     pl.semaphore_wait(barrier, len(partners))
@@ -967,10 +966,13 @@
     def close(i, carry):
         rows = tile(i, 256)
         branch = dot(hidden[rows, :], outer_w[...])
-        result = middle[rows, :] + branch
+        mid = middle[rows, :]
+        first = mid - tokens[rows, :].astype(F32)
+        result = mid + branch
         grad_query[rows, :] = result.astype(BF)
         valid = jnp.where(segment_column[rows, 0:1] < ITEMS_ROW, 1.0, 0.0)
         small_ref[2:3, :] += jnp.sum(valid * result * result, axis=0, keepdims=True)
+        small_ref[3:4, :] += jnp.sum(valid * first * first, axis=0, keepdims=True)
         small_ref[4:5, :] += jnp.sum(valid * branch * branch, axis=0, keepdims=True)
         return carry
 

time: 140 us -> 139 us (level)
  no operation moved by 1% of the time
where the time goes in v2:
time: 139 us
  Pallas kernels  138 us (99%)
    pallas_call x1, Pallas kernels, fast_shards(): pl.pallas_call(layer_kernel, out_shape=[shape((1024, 512), BF), shape((10...  127 us
    pallas_call x1, Pallas kernels, fast_shards(): pl.pallas_call(closing_kernel, out_shape=[shape((1024, 512), BF), shape((...  11.6 us

profile of v2, /device:TPU:0, one launch (start us, length us, event | category | flops | bytes accessed | tf_op | source)
XLA Modules:
  0.0 139.2 jit_solution(14441226997827655384)
XLA Ops:
  0.6 126.8 %shard_map.219 = (bf16[1024,512]{1,0:T(8,128)(2,1)}, bf16[1024,512]{1,0:T(8,128)(2,1)}, f32[32,512,128]{2,1,0:T(8,128)}, f32[2,2,4,2,2,8,2048]{6,5,4,3,2,1,0:T(8...) custom-call(bf16[1024,512]{1,0:T(8,128)(2,1)} %bitcast.9, s32[2,512]{1,0:T(2,128)} %bitcast.10, ...), custom_call_target="tpu_custom_call" | custom-call | tf_op jit(solution)/shard_map/pallas_call | solution.py:1306
  127.4 11.6 %shard_map.220 = (bf16[1024,512]{1,0:T(8,128)(2,1)}, bf16[1024,512]{1,0:T(8,128)(2,1)}, f32[512]{0:T(512)}, f32[512,512]{1,0:T(8,128)}, f32[512,512]{1,0:T(8,128...) custom-call(bf16[1024,512]{1,0:T(8,128)(2,1)} %get-tuple-element.32., ...), custom_call_target="tpu_custom_call" | custom-call | tf_op jit(solution)/shard_map/pallas_call | solution.py:1388

commit v3 on v2

--- a/solution.py
+++ b/solution.py
@@ -1249,7 +1249,9 @@
         pltpu.make_async_copy(source, target, load_sem.at[i])
         for i, (source, target) in enumerate(pairs)
     ]
-    for load in loads:
+    quarter = UNITS // 4
+    early = loads[2 : 2 + quarter]
+    for load in early + loads[:2] + loads[2 + quarter :]:
         load.start()
     gain_one_out[...] = small_ref[0, :]
     gain_two_out[...] = small_ref[1, :]
@@ -1260,6 +1262,9 @@
     roots = jnp.sqrt(squares / valid)
     for i in range(3):
         square_out[i] = jnp.max(roots[i : i + 1, :])
+    for i in range(quarter):
+        loads[2 + i].wait()
+        copies[i].start()
     loads[0].wait()
     loads[1].wait()
     hidden_low[...] = hidden_sum[...].reshape(512, 2048).astype(BF)
@@ -1271,7 +1276,7 @@
         store = pltpu.make_async_copy(outer_part.at[rows], outer_out.at[rows], store_sem.at[c])
         store.start()
         stores.append(store)
-        for i in range(UNITS // 4 * c, UNITS // 4 * (c + 1)):
+        for i in range(quarter * (c + 1), min(quarter * (c + 2), UNITS)):
             loads[2 + i].wait()
             copies[i].start()
     for i in (UNITS, UNITS + 1):

time: 139 us -> 139 us (level)
  no operation moved by 1% of the time
where the time goes in v3:
time: 139 us
  Pallas kernels  138 us (99%)
    pallas_call x1, Pallas kernels, fast_shards(): pl.pallas_call(layer_kernel, out_shape=[shape((1024, 512), BF), shape((10...  127 us
    pallas_call x1, Pallas kernels, fast_shards(): pl.pallas_call(closing_kernel, out_shape=[shape((1024, 512), BF), shape((...  11.2 us

profile of v3, /device:TPU:0, one launch (start us, length us, event | category | flops | bytes accessed | tf_op | source)
XLA Modules:
  0.0 138.8 jit_solution(9480208208817269699)
XLA Ops:
  0.6 126.8 %shard_map.219 = (bf16[1024,512]{1,0:T(8,128)(2,1)}, bf16[1024,512]{1,0:T(8,128)(2,1)}, f32[32,512,128]{2,1,0:T(8,128)}, f32[2,2,4,2,2,8,2048]{6,5,4,3,2,1,0:T(8...) custom-call(bf16[1024,512]{1,0:T(8,128)(2,1)} %bitcast.9, s32[2,512]{1,0:T(2,128)} %bitcast.10, ...), custom_call_target="tpu_custom_call" | custom-call | tf_op jit(solution)/shard_map/pallas_call | solution.py:1311
  127.4 11.2 %shard_map.220 = (bf16[1024,512]{1,0:T(8,128)(2,1)}, bf16[1024,512]{1,0:T(8,128)(2,1)}, f32[512]{0:T(512)}, f32[512,512]{1,0:T(8,128)}, f32[512,512]{1,0:T(8,128...) custom-call(bf16[1024,512]{1,0:T(8,128)(2,1)} %get-tuple-element.32., ...), custom_call_target="tpu_custom_call" | custom-call | tf_op jit(solution)/shard_map/pallas_call | solution.py:1393
